TPU v7x, 32 devices: a whole 2x2x4 slice. The times are simulated.
32 devices in a mesh: head: 4 (over x, core), ctx: 8 (over z, y).
Axes of the slice: x: 2, y: 2, z: 4, core: 2. Of those that a mesh axis runs over, the one named last changes fastest.
Arguments:
- query_rows: bfloat16 [3072, 16, 128], P(('ctx', 'head')), may hold values from -1.6953125 to 1.6953125
- key_matrix: bfloat16 [3072, 1, 128], P(('ctx', 'head')), may hold values from -1.6953125 to 1.6953125
- value_matrix: bfloat16 [3072, 1, 128], P(('ctx', 'head')), may hold values from -6 to 6
- output_rows: bfloat16 [3072, 16, 128], P(('ctx', 'head')), may hold values from -3 to 3
- out_grad: bfloat16 [3072, 16, 128], P(('ctx', 'head')), may hold values from -6 to 6
- log_norm: float32 [3072, 16], P(('ctx', 'head')), as said below
- span_order: int32 [16], replicated, may hold values from 0 to 15, as said below
Outputs:
- query_grad: bfloat16 [3072, 16, 128], P(('ctx', 'head'))
- key_grad: bfloat16 [3072, 1, 128], P(('ctx', 'head'))
- value_grad: bfloat16 [3072, 1, 128], P(('ctx', 'head'))
Inputs may be any that keep to these rules, and one draw needn't show every extreme that they name: A permutation of 0 to 15: stored span j of every token-indexed array holds the tokens of sequence span span_order[j]. `log_norm`: the normalizers of the forward pass in the log domain, of the size of the logarithm of the row's position in the sequence.
All inputs are finite; a program needn't handle non-finite values.
Results may differ from a plain program's by a relative error of at most 0.0051.
Values may be sent and summed in bfloat16 or wider, within the bound.
A program may use at most 64 MiB of HBM per device.

v0:
```python
import jax
import jax.numpy as jnp
from jax import lax
from jax.sharding import PartitionSpec as P


def passed_along(value, axis, steps):
    count = lax.axis_size(axis)
    pairs = [(source, (source + steps) % count) for source in range(count)]
    return lax.ppermute(value, axis, pairs)


def pair_grads(queries, grads_out, lse_rows, delta_rows, key_block, value_block, allowed):
    head_size = queries.shape[-1]
    logit_scores = jnp.einsum(
        "qhd,kd->qhk", queries, key_block, preferred_element_type=jnp.float32
    ) * head_size ** (-0.5)
    shifted = logit_scores - lse_rows[:, :, None]
    if allowed is not None:
        shifted = jnp.where(allowed[:, None, :], shifted, -jnp.inf)
    soft_probs = jnp.exp(shifted)
    probs_b = soft_probs.astype(jnp.bfloat16)
    value_part = jnp.einsum("qhk,qhd->kd", probs_b, grads_out, preferred_element_type=jnp.float32)
    prob_grads = jnp.einsum(
        "qhd,kd->qhk", grads_out, value_block, preferred_element_type=jnp.float32
    )
    score_grads = (soft_probs * (prob_grads - delta_rows[:, :, None])).astype(jnp.bfloat16)
    query_part = jnp.einsum(
        "qhk,kd->qhd", score_grads, key_block, preferred_element_type=jnp.float32
    )
    key_part = jnp.einsum("qhk,qhd->kd", score_grads, queries, preferred_element_type=jnp.float32)
    return (query_part, key_part, value_part)


def local(query_rows, key_matrix, value_matrix, output_rows, out_grad, log_norm, span_order):
    f32 = jnp.float32
    head_count = lax.axis_size("head")
    cycle_size = lax.axis_size("ctx")
    cycle_pos = lax.axis_index("ctx")
    queries, outputs, grads_out = (
        lax.all_to_all(query_rows, "head", split_axis=1, concat_axis=0, tiled=True),
        lax.all_to_all(output_rows, "head", split_axis=1, concat_axis=0, tiled=True),
        lax.all_to_all(out_grad, "head", split_axis=1, concat_axis=0, tiled=True),
    )
    lse_local = lax.all_to_all(log_norm, "head", split_axis=1, concat_axis=0, tiled=True)
    delta_local = jnp.sum(outputs.astype(f32) * grads_out.astype(f32), axis=-1)
    kv_heads = key_matrix.shape[1]
    spread = head_count // kv_heads
    key_local, value_local = (
        lax.all_to_all(
            jnp.repeat(key_matrix, spread, axis=1), "head", split_axis=1, concat_axis=0, tiled=True
        ),
        lax.all_to_all(
            jnp.repeat(value_matrix, spread, axis=1),
            "head",
            split_axis=1,
            concat_axis=0,
            tiled=True,
        ),
    )
    key_local = key_local[:, 0, :]
    value_local = value_local[:, 0, :]
    local_rows = queries.shape[0]
    span_len = local_rows // 2
    offsets = jnp.arange(span_len, dtype=jnp.int32)

    def span_ids(owner):
        return lax.dynamic_slice_in_dim(span_order, 2 * owner, 2)

    query_spans = span_ids(cycle_pos)
    inner = offsets[None, :] <= offsets[:, None]

    def skipped(query_blk, grads_blk, lse_blk, delta_blk, key_blk, value_blk):
        return (
            jnp.zeros(query_blk.shape, f32),
            jnp.zeros(key_blk.shape, f32),
            jnp.zeros(key_blk.shape, f32),
        )

    def diagonal(query_blk, grads_blk, lse_blk, delta_blk, key_blk, value_blk):
        return pair_grads(query_blk, grads_blk, lse_blk, delta_blk, key_blk, value_blk, inner)

    def complete(query_blk, grads_blk, lse_blk, delta_blk, key_blk, value_blk):
        return pair_grads(query_blk, grads_blk, lse_blk, delta_blk, key_blk, value_blk, None)

    def contributions(key_block, value_block, owner):
        key_spans = span_ids(owner)
        query_halves = []
        key_halves = [jnp.zeros((span_len,) + key_block.shape[1:], f32) for key_half in range(2)]
        value_halves = [jnp.zeros((span_len,) + key_block.shape[1:], f32) for key_half in range(2)]
        for query_half in range(2):
            low_q = query_half * span_len
            query_total = jnp.zeros((span_len,) + queries.shape[1:], f32)
            for key_half in range(2):
                low_k = key_half * span_len
                relation = jnp.where(
                    query_spans[query_half] > key_spans[key_half],
                    2,
                    jnp.where(query_spans[query_half] == key_spans[key_half], 1, 0),
                )
                query_part, key_part, value_part = lax.switch(
                    relation,
                    (skipped, diagonal, complete),
                    queries[low_q : low_q + span_len],
                    grads_out[low_q : low_q + span_len],
                    lse_local[low_q : low_q + span_len],
                    delta_local[low_q : low_q + span_len],
                    key_block[low_k : low_k + span_len],
                    value_block[low_k : low_k + span_len],
                )
                query_total = query_total + query_part
                key_halves[key_half] = key_halves[key_half] + key_part
                value_halves[key_half] = value_halves[key_half] + value_part
            query_halves.append(query_total)
        return (
            jnp.concatenate(query_halves, axis=0),
            jnp.concatenate(key_halves, axis=0),
            jnp.concatenate(value_halves, axis=0),
        )

    def turn(turn_index, carry):
        key_block, value_block, key_acc, value_acc, query_acc = carry
        owner = (cycle_pos - turn_index) % cycle_size
        query_part, key_part, value_part = contributions(key_block, value_block, owner)
        key_block, value_block = passed_along((key_block, value_block), "ctx", 1)
        key_acc, value_acc = passed_along((key_acc + key_part, value_acc + value_part), "ctx", 1)
        return (key_block, value_block, key_acc, value_acc, query_acc + query_part)

    def two_turns(loop_index, carry):
        return turn(2 * loop_index + 1, turn(2 * loop_index, carry))

    zeros_query = jnp.zeros(queries.shape, f32)
    start_accs = (jnp.zeros(key_local.shape, f32), jnp.zeros(key_local.shape, f32))
    final = lax.fori_loop(
        0, cycle_size // 2, two_turns, (key_local, value_local) + start_accs + (zeros_query,)
    )
    key_sum, value_sum = (final[2], final[3])
    scale = key_local.shape[-1] ** (-0.5)
    query_grad = (final[4] * scale).astype(jnp.bfloat16)
    query_grad = lax.all_to_all(query_grad, "head", split_axis=0, concat_axis=1, tiled=True)
    picker = (jnp.arange(kv_heads, dtype=jnp.int32) == lax.axis_index("head") // spread).astype(f32)
    expanded_keys = key_sum[:, None, :] * picker[None, :, None]
    value_full = value_sum[:, None, :] * picker[None, :, None]
    key_total, value_total = (
        lax.psum_scatter(expanded_keys, "head", scatter_dimension=0, tiled=True),
        lax.psum_scatter(value_full, "head", scatter_dimension=0, tiled=True),
    )
    key_grad = (key_total * scale).astype(jnp.bfloat16)
    value_grad = value_total.astype(jnp.bfloat16)
    return (query_grad, key_grad, value_grad)


def solution(mesh):
    in_specs = (
        P(("ctx", "head"), None, None),
        P(("ctx", "head"), None, None),
        P(("ctx", "head"), None, None),
        P(("ctx", "head"), None, None),
        P(("ctx", "head"), None, None),
        P(("ctx", "head"), None),
        P(),
    )
    out_specs = (
        P(("ctx", "head"), None, None),
        P(("ctx", "head"), None, None),
        P(("ctx", "head"), None, None),
    )
    return jax.shard_map(local, mesh=mesh, in_specs=in_specs, out_specs=out_specs, check_vma=False)
```

profile of v0, /device:TPU:0, one launch (start us, length us, event | category | flops | bytes accessed | tf_op | source)
XLA Modules:
  0.0 368.7 jit_solution(17074747572304091782)
XLA Ops:
  7.2 8.0 %all_to_all.112 = f32[96,4,4]{0,2,1:T(4,128)S(1)} all-to-all(f32[96,4,4]{0,2,1:T(4,128)} %bitcast.363), channel_id=1, replica_groups=mesh['head'=4,'ctx'=8] {'head'}, dimensions={1} | all-to-all | bytes 12288 | tf_op jit(solution)/shard_map/all_to_all | solution.py:45
  16.6 3.9 %all-to-all-start = ((bf16[96,4,128]{2,0,1:T(8,128)(2,1)}), bf16[96,4,128]{2,0,1:T(8,128)(2,1)}, u32[]{:S(2)}, u32[]{:S(2)}) async-start(bf16[96,4,128]{2,0,1:T(8,128)(2,1)} %reshape.151), calls=%async_computation | async-start | bytes 196608 | tf_op jit(solution)/shard_map/all_to_all | solution.py:50
  20.5 1.8 copy.239
  22.4 2.5 all-to-all-done
  24.9 3.5 all-to-all-start.2
  29.2 6.5 %all-to-all-done.2 = bf16[96,16,128]{2,0,1:T(8,128)(2,1)S(1)} async-done(((bf16[96,16,128]{2,0,1:T(8,128)(2,1)}), bf16[96,16,128]{2,0,1:T(8,128)(2,1)S(1)}, u32[]{:S(2)}, u32[]{:S(2)}) %all-to-all-start.2) | async-done | bytes 393248 | tf_op jit(solution)/shard_map/all_to_all | solution.py:41
  35.7 3.5 all-to-all-start.5
  40.1 6.5 %all-to-all-done.5 = bf16[96,16,128]{2,0,1:T(8,128)(2,1)S(1)} async-done(((bf16[96,16,128]{2,0,1:T(8,128)(2,1)}), bf16[96,16,128]{2,0,1:T(8,128)(2,1)S(1)}, u32[]{:S(2)}, u32[]{:S(2)}) %all-to-all-start.5) | async-done | bytes 393248 | tf_op jit(solution)/shard_map/all_to_all | solution.py:42
  46.6 3.5 all-to-all-start.4
  50.9 6.5 %all-to-all-done.4 = bf16[96,16,128]{2,0,1:T(8,128)(2,1)S(1)} async-done(((bf16[96,16,128]{2,0,1:T(8,128)(2,1)}), bf16[96,16,128]{2,0,1:T(8,128)(2,1)S(1)}, u32[]{:S(2)}, u32[]{:S(2)}) %all-to-all-start.4) | async-done | bytes 393248 | tf_op jit(solution)/shard_map/all_to_all | solution.py:43
  58.1 3.9 %all-to-all-start.1 = ((bf16[96,4,128]{2,0,1:T(8,128)(2,1)}), bf16[96,4,128]{2,0,1:T(8,128)(2,1)}, u32[]{:S(2)}, u32[]{:S(2)}) async-start(bf16[96,4,128]{2,0,1:T(8,128)(2,1)} %reshape.152), calls=%async_computation.1 | async-start | bytes 196608 | tf_op jit(solution)/shard_map/all_to_all | solution.py:53
  64.1 2.3 all-to-all-done.1
  67.8 249.5 %while.25 = (s32[]{:T(128)}, bf16[384,128]{1,0:T(8,128)(2,1)}, bf16[384,128]{1,0:T(8,128)(2,1)}, f32[384,128]{1,0:T(8,128)}, f32[384,128]{1,0:T(8,128)}, /*index...) while((s32[]{:T(128)}, bf16[384,128]{1,0:T(8,128)(2,1)}, ...), condition=%wide.region_26.27_spmd.clone.clone, body=%wide.region_1.26_spmd.clone.clone.sunk | while | flops 1520209920 | bytes 57326844 | solution.py:134
  67.8 2.0 collective-permute-start
  69.8 1.5 collective-permute-start.2
  90.2 1.7 maximum_add_fusion.11
  94.3 1.6 maximum_add_fusion.9
  95.9 1.5 collective-permute-start.4
  114.1 5.6 %collective-permute-start.1 = (bf16[384,128]{1,0:T(8,128)(2,1)}, bf16[384,128]{1,0:T(8,128)(2,1)}, u32[]{:S(2)}, u32[]{:S(2)}) collective-permute-start(bf16[384,128]{1,0:T(8,128)(2,1)} %collective-permute-done), channel_id=1, source_target_pairs={{0,1},{1,2},{2,3},{3,4},{4,5},{5,6},{6,7},{7,0},{8,9},{9,10},{10,1... | collective-permute-start | bytes 294920 | tf_op jit(solution)/shard_map/while/body/eval_jaxpr/ppermute | solution.py:10
  120.7 1.7 collective-permute-start.7
  124.0 4.4 %collective-permute-done.3 = bf16[384,128]{1,0:T(8,128)(2,1)} collective-permute-done((bf16[384,128]{1,0:T(8,128)(2,1)}, bf16[384,128]{1,0:T(8,128)(2,1)}, u32[]{:S(2)}, u32[]{:S(2)}) %collective-permute-start.3) | collective-permute-done | bytes 98336 | tf_op jit(solution)/shard_map/while/body/eval_jaxpr/ppermute | solution.py:10
  128.4 3.5 collective-permute-done.7
  131.9 2.1 collective-permute-done.5
  153.1 1.7 maximum_add_fusion.11
  154.8 1.8 collective-permute-start.6
  157.5 1.6 maximum_add_fusion.9
  182.5 2.6 collective-permute-start.7
  187.7 2.3 collective-permute-done.1
  191.5 2.1 collective-permute-done.7
  193.6 2.1 collective-permute-done.5
  214.4 1.7 maximum_add_fusion.11
  216.0 2.9 collective-permute-start.6
  219.8 1.6 maximum_add_fusion.9
  236.9 6.2 %collective-permute-start.1 = (bf16[384,128]{1,0:T(8,128)(2,1)}, bf16[384,128]{1,0:T(8,128)(2,1)}, u32[]{:S(2)}, u32[]{:S(2)}) collective-permute-start(bf16[384,128]{1,0:T(8,128)(2,1)} %collective-permute-done), channel_id=1, source_target_pairs={{0,1},{1,2},{2,3},{3,4},{4,5},{5,6},{6,7},{7,0},{8,9},{9,10},{10,1... | collective-permute-start | bytes 294920 | tf_op jit(solution)/shard_map/while/body/eval_jaxpr/ppermute | solution.py:10
  243.2 2.7 collective-permute-start.3
  249.5 2.5 collective-permute-done.3
  251.9 3.4 collective-permute-done.7
  255.3 2.1 collective-permute-done.5
  275.5 1.7 maximum_add_fusion.11
  279.5 1.6 maximum_add_fusion.9
  297.3 7.2 %collective-permute-start.1 = (bf16[384,128]{1,0:T(8,128)(2,1)}, bf16[384,128]{1,0:T(8,128)(2,1)}, u32[]{:S(2)}, u32[]{:S(2)}) collective-permute-start(bf16[384,128]{1,0:T(8,128)(2,1)} %collective-permute-done), channel_id=1, source_target_pairs={{0,1},{1,2},{2,3},{3,4},{4,5},{5,6},{6,7},{7,0},{8,9},{9,10},{10,1... | collective-permute-start | bytes 294920 | tf_op jit(solution)/shard_map/while/body/eval_jaxpr/ppermute | solution.py:10
  306.6 6.8 %collective-permute-start.5 = (f32[384,128]{1,0:T(8,128)S(1)}, f32[384,128]{1,0:T(8,128)}, u32[]{:S(2)}, u32[]{:S(2)}) collective-permute-start(f32[384,128]{1,0:T(8,128)S(1)} %maximum_add_fusion.10), channel_id=1, source_target_pairs={{0,1},{1,2},{2,3},{3,4},{4,5},{5,6},{6,7},{7,0},{8,9},{9,10},{10,1... | collective-permute-start | bytes 589832 | tf_op jit(solution)/shard_map/while/body/eval_jaxpr/ppermute | solution.py:10
  314.3 2.3 collective-permute-done.5
  317.3 1.6 multiply_bitcast_fusion
  318.9 1.6 multiply_bitcast_fusion.1
  321.0 9.8 %all_to_all.113 = bf16[384,4,128]{2,1,0:T(4,128)(2,1)S(1)} all-to-all(bf16[384,4,128]{2,1,0:T(4,128)(2,1)S(1)} %copy.246), channel_id=1, replica_groups=mesh['head'=4,'ctx'=8] {'head'}, dimensions={0} | all-to-all | bytes 786432 | tf_op jit(solution)/shard_map/all_to_all | solution.py:140
  331.7 6.5 %reduce-scatter.5.cloned.1.call-done = f32[96,1,128]{2,0,1:T(8,128)} async-done(((f32[384,1,128]{2,0,1:T(8,128)}), f32[96,1,128]{2,0,1:T(8,128)}) %reduce-scatter.5.cloned.1.call-update) | async-done | bytes 49168 | tf_op jit(solution)/shard_map/reduce_scatter | solution.py:146
  339.6 20.8 %reduce-scatter.3.cloned.1.call-done = f32[96,1,128]{2,0,1:T(8,128)} async-done(((f32[384,1,128]{2,0,1:T(8,128)}), f32[96,1,128]{2,0,1:T(8,128)}) %reduce-scatter.3.cloned.1.call-update) | async-done | bytes 49168 | tf_op jit(solution)/shard_map/reduce_scatter | solution.py:145
  (476 shorter events, 120.5 us)
Async XLA Ops:
  16.6 8.3 %all-to-all-start = ((bf16[96,4,128]{2,0,1:T(8,128)(2,1)}), bf16[96,4,128]{2,0,1:T(8,128)(2,1)}, u32[]{:S(2)}, u32[]{:S(2)}) async-start(bf16[96,4,128]{2,0,1:T(8,128)(2,1)} %reshape.151), calls=%async_computation | async-start | bytes 196608 | tf_op jit(solution)/shard_map/all_to_all | solution.py:50
  24.9 10.9 %all-to-all-start.2 = ((bf16[96,16,128]{2,0,1:T(8,128)(2,1)}), bf16[96,16,128]{2,0,1:T(8,128)(2,1)S(1)}, u32[]{:S(2)}, u32[]{:S(2)}) async-start(bf16[96,16,128]{2,0,1:T(8,128)(2,1)} %copy.239), calls=%async_computation.2 | async-start | bytes 786432 | tf_op jit(solution)/shard_map/all_to_all | solution.py:41
  35.7 10.9 %all-to-all-start.5 = ((bf16[96,16,128]{2,0,1:T(8,128)(2,1)}), bf16[96,16,128]{2,0,1:T(8,128)(2,1)S(1)}, u32[]{:S(2)}, u32[]{:S(2)}) async-start(bf16[96,16,128]{2,0,1:T(8,128)(2,1)} %copy.244), calls=%async_computation.5 | async-start | bytes 786432 | tf_op jit(solution)/shard_map/all_to_all | solution.py:42
  46.6 10.9 %all-to-all-start.4 = ((bf16[96,16,128]{2,0,1:T(8,128)(2,1)}), bf16[96,16,128]{2,0,1:T(8,128)(2,1)S(1)}, u32[]{:S(2)}, u32[]{:S(2)}) async-start(bf16[96,16,128]{2,0,1:T(8,128)(2,1)} %copy.242), calls=%async_computation.4 | async-start | bytes 786432 | tf_op jit(solution)/shard_map/all_to_all | solution.py:43
  58.1 8.3 %all-to-all-start.1 = ((bf16[96,4,128]{2,0,1:T(8,128)(2,1)}), bf16[96,4,128]{2,0,1:T(8,128)(2,1)}, u32[]{:S(2)}, u32[]{:S(2)}) async-start(bf16[96,4,128]{2,0,1:T(8,128)(2,1)} %reshape.152), calls=%async_computation.1 | async-start | bytes 196608 | tf_op jit(solution)/shard_map/all_to_all | solution.py:53
  62.1 276.2 %reduce-scatter.5.cloned.1.call-start = ((), (), s32[]{:S(2)}) async-start(), calls=%async_computation.10 | async-start | bytes 245760 | tf_op jit(solution)/shard_map/reduce_scatter | solution.py:146
  67.8 15.2 %copy-start.14 = (f32[384,4]{0,1:T(4,128)}, f32[384,4]{0,1:T(4,128)S(1)}, u32[]{:S(2)}) copy-start(f32[384,4]{0,1:T(4,128)S(1)} %get-tuple-element.1185) | copy-start | bytes 18436 | tf_op jit(solution)/shard_map/while
  67.8 15.2 %copy-start.16 = (f32[384,4]{0,1:T(4,128)}, f32[384,4]{0,1:T(4,128)S(1)}, u32[]{:S(2)}) copy-start(f32[384,4]{0,1:T(4,128)S(1)} %get-tuple-element.1187) | copy-start | bytes 18436 | tf_op jit(solution)/shard_map/while
  67.8 39.4 %collective-permute-start = (bf16[384,128]{1,0:T(8,128)(2,1)}, bf16[384,128]{1,0:T(8,128)(2,1)}, u32[]{:S(2)}, u32[]{:S(2)}) collective-permute-start(bf16[384,128]{1,0:T(8,128)(2,1)} %get-tuple-element.1154), channel_id=1, source_target_pairs={{0,1},{1,2},{2,3},{3,4},{4,5},{5,6},{6,7},{7,0},{8,9},{9,10},{10,1... | collective-permute-start | bytes 294920 | tf_op jit(solution)/shard_map/while/body/eval_jaxpr/ppermute | solution.py:10
  69.8 38.2 %collective-permute-start.2 = (bf16[384,128]{1,0:T(8,128)(2,1)}, bf16[384,128]{1,0:T(8,128)(2,1)}, u32[]{:S(2)}, u32[]{:S(2)}) collective-permute-start(bf16[384,128]{1,0:T(8,128)(2,1)} %get-tuple-element.1155), channel_id=1, source_target_pairs={{0,1},{1,2},{2,3},{3,4},{4,5},{5,6},{6,7},{7,0},{8,9},{9,10},{10,1... | collective-permute-start | bytes 294920 | tf_op jit(solution)/shard_map/while/body/eval_jaxpr/ppermute | solution.py:10
  91.9 27.9 %collective-permute-start.6 = (f32[384,128]{1,0:T(8,128)}, f32[384,128]{1,0:T(8,128)}, u32[]{:S(2)}, u32[]{:S(2)}) collective-permute-start(f32[384,128]{1,0:T(8,128)} %maximum_add_fusion.11), channel_id=1, source_target_pairs={{0,1},{1,2},{2,3},{3,4},{4,5},{5,6},{6,7},{7,0},{8,9},{9,10},{10,1... | collective-permute-start | bytes 589832 | tf_op jit(solution)/shard_map/while/body/eval_jaxpr/ppermute | solution.py:10
  95.9 26.5 %collective-permute-start.4 = (f32[384,128]{1,0:T(8,128)}, f32[384,128]{1,0:T(8,128)}, u32[]{:S(2)}, u32[]{:S(2)}) collective-permute-start(f32[384,128]{1,0:T(8,128)} %maximum_add_fusion.9), channel_id=1, source_target_pairs={{0,1},{1,2},{2,3},{3,4},{4,5},{5,6},{6,7},{7,0},{8,9},{9,10},{10,1... | collective-permute-start | bytes 589832 | tf_op jit(solution)/shard_map/while/body/eval_jaxpr/ppermute | solution.py:10
  114.1 9.9 %collective-permute-start.1 = (bf16[384,128]{1,0:T(8,128)(2,1)}, bf16[384,128]{1,0:T(8,128)(2,1)}, u32[]{:S(2)}, u32[]{:S(2)}) collective-permute-start(bf16[384,128]{1,0:T(8,128)(2,1)} %collective-permute-done), channel_id=1, source_target_pairs={{0,1},{1,2},{2,3},{3,4},{4,5},{5,6},{6,7},{7,0},{8,9},{9,10},{10,1... | collective-permute-start | bytes 294920 | tf_op jit(solution)/shard_map/while/body/eval_jaxpr/ppermute | solution.py:10
  119.7 8.7 %collective-permute-start.3 = (bf16[384,128]{1,0:T(8,128)(2,1)}, bf16[384,128]{1,0:T(8,128)(2,1)}, u32[]{:S(2)}, u32[]{:S(2)}) collective-permute-start(bf16[384,128]{1,0:T(8,128)(2,1)} %collective-permute-done.2), channel_id=1, source_target_pairs={{0,1},{1,2},{2,3},{3,4},{4,5},{5,6},{6,7},{7,0},{8,9},{9,10},{10,1... | collective-permute-start | bytes 294920 | tf_op jit(solution)/shard_map/while/body/eval_jaxpr/ppermute | solution.py:10
  120.7 11.2 %collective-permute-start.7 = (f32[384,128]{1,0:T(8,128)S(1)}, f32[384,128]{1,0:T(8,128)}, u32[]{:S(2)}, u32[]{:S(2)}) collective-permute-start(f32[384,128]{1,0:T(8,128)S(1)} %maximum_add_fusion.12), channel_id=1, source_target_pairs={{0,1},{1,2},{2,3},{3,4},{4,5},{5,6},{6,7},{7,0},{8,9},{9,10},{10,1... | collective-permute-start | bytes 589832 | tf_op jit(solution)/shard_map/while/body/eval_jaxpr/ppermute | solution.py:10
  123.4 10.6 %collective-permute-start.5 = (f32[384,128]{1,0:T(8,128)S(1)}, f32[384,128]{1,0:T(8,128)}, u32[]{:S(2)}, u32[]{:S(2)}) collective-permute-start(f32[384,128]{1,0:T(8,128)S(1)} %maximum_add_fusion.10), channel_id=1, source_target_pairs={{0,1},{1,2},{2,3},{3,4},{4,5},{5,6},{6,7},{7,0},{8,9},{9,10},{10,1... | collective-permute-start | bytes 589832 | tf_op jit(solution)/shard_map/while/body/eval_jaxpr/ppermute | solution.py:10
  123.5 10.5 %copy-start.17 = (f32[384,4]{0,1:T(4,128)S(1)}, f32[384,4]{0,1:T(4,128)}, u32[]{:S(2)}) copy-start(f32[384,4]{0,1:T(4,128)} %copy-done.16) | copy-start | bytes 18436 | tf_op jit(solution)/shard_map/while
  134.7 12.7 %copy-start.14 = (f32[384,4]{0,1:T(4,128)}, f32[384,4]{0,1:T(4,128)S(1)}, u32[]{:S(2)}) copy-start(f32[384,4]{0,1:T(4,128)S(1)} %get-tuple-element.1185) | copy-start | bytes 18436 | tf_op jit(solution)/shard_map/while
  134.7 12.7 %copy-start.16 = (f32[384,4]{0,1:T(4,128)}, f32[384,4]{0,1:T(4,128)S(1)}, u32[]{:S(2)}) copy-start(f32[384,4]{0,1:T(4,128)S(1)} %get-tuple-element.1187) | copy-start | bytes 18436 | tf_op jit(solution)/shard_map/while
  134.7 35.7 %collective-permute-start = (bf16[384,128]{1,0:T(8,128)(2,1)}, bf16[384,128]{1,0:T(8,128)(2,1)}, u32[]{:S(2)}, u32[]{:S(2)}) collective-permute-start(bf16[384,128]{1,0:T(8,128)(2,1)} %get-tuple-element.1154), channel_id=1, source_target_pairs={{0,1},{1,2},{2,3},{3,4},{4,5},{5,6},{6,7},{7,0},{8,9},{9,10},{10,1... | collective-permute-start | bytes 294920 | tf_op jit(solution)/shard_map/while/body/eval_jaxpr/ppermute | solution.py:10
  134.7 36.5 %collective-permute-start.2 = (bf16[384,128]{1,0:T(8,128)(2,1)}, bf16[384,128]{1,0:T(8,128)(2,1)}, u32[]{:S(2)}, u32[]{:S(2)}) collective-permute-start(bf16[384,128]{1,0:T(8,128)(2,1)} %get-tuple-element.1155), channel_id=1, source_target_pairs={{0,1},{1,2},{2,3},{3,4},{4,5},{5,6},{6,7},{7,0},{8,9},{9,10},{10,1... | collective-permute-start | bytes 294920 | tf_op jit(solution)/shard_map/while/body/eval_jaxpr/ppermute | solution.py:10
  154.8 26.7 %collective-permute-start.6 = (f32[384,128]{1,0:T(8,128)}, f32[384,128]{1,0:T(8,128)}, u32[]{:S(2)}, u32[]{:S(2)}) collective-permute-start(f32[384,128]{1,0:T(8,128)} %maximum_add_fusion.11), channel_id=1, source_target_pairs={{0,1},{1,2},{2,3},{3,4},{4,5},{5,6},{6,7},{7,0},{8,9},{9,10},{10,1... | collective-permute-start | bytes 589832 | tf_op jit(solution)/shard_map/while/body/eval_jaxpr/ppermute | solution.py:10
  159.1 25.9 %collective-permute-start.4 = (f32[384,128]{1,0:T(8,128)}, f32[384,128]{1,0:T(8,128)}, u32[]{:S(2)}, u32[]{:S(2)}) collective-permute-start(f32[384,128]{1,0:T(8,128)} %maximum_add_fusion.9), channel_id=1, source_target_pairs={{0,1},{1,2},{2,3},{3,4},{4,5},{5,6},{6,7},{7,0},{8,9},{9,10},{10,1... | collective-permute-start | bytes 589832 | tf_op jit(solution)/shard_map/while/body/eval_jaxpr/ppermute | solution.py:10
  181.4 8.7 %collective-permute-start.1 = (bf16[384,128]{1,0:T(8,128)(2,1)}, bf16[384,128]{1,0:T(8,128)(2,1)}, u32[]{:S(2)}, u32[]{:S(2)}) collective-permute-start(bf16[384,128]{1,0:T(8,128)(2,1)} %collective-permute-done), channel_id=1, source_target_pairs={{0,1},{1,2},{2,3},{3,4},{4,5},{5,6},{6,7},{7,0},{8,9},{9,10},{10,1... | collective-permute-start | bytes 294920 | tf_op jit(solution)/shard_map/while/body/eval_jaxpr/ppermute | solution.py:10
  181.4 10.1 %collective-permute-start.3 = (bf16[384,128]{1,0:T(8,128)(2,1)}, bf16[384,128]{1,0:T(8,128)(2,1)}, u32[]{:S(2)}, u32[]{:S(2)}) collective-permute-start(bf16[384,128]{1,0:T(8,128)(2,1)} %collective-permute-done.2), channel_id=1, source_target_pairs={{0,1},{1,2},{2,3},{3,4},{4,5},{5,6},{6,7},{7,0},{8,9},{9,10},{10,1... | collective-permute-start | bytes 294920 | tf_op jit(solution)/shard_map/while/body/eval_jaxpr/ppermute | solution.py:10
  182.5 11.1 %collective-permute-start.7 = (f32[384,128]{1,0:T(8,128)S(1)}, f32[384,128]{1,0:T(8,128)}, u32[]{:S(2)}, u32[]{:S(2)}) collective-permute-start(f32[384,128]{1,0:T(8,128)S(1)} %maximum_add_fusion.12), channel_id=1, source_target_pairs={{0,1},{1,2},{2,3},{3,4},{4,5},{5,6},{6,7},{7,0},{8,9},{9,10},{10,1... | collective-permute-start | bytes 589832 | tf_op jit(solution)/shard_map/while/body/eval_jaxpr/ppermute | solution.py:10
  186.0 9.7 %collective-permute-start.5 = (f32[384,128]{1,0:T(8,128)S(1)}, f32[384,128]{1,0:T(8,128)}, u32[]{:S(2)}, u32[]{:S(2)}) collective-permute-start(f32[384,128]{1,0:T(8,128)S(1)} %maximum_add_fusion.10), channel_id=1, source_target_pairs={{0,1},{1,2},{2,3},{3,4},{4,5},{5,6},{6,7},{7,0},{8,9},{9,10},{10,1... | collective-permute-start | bytes 589832 | tf_op jit(solution)/shard_map/while/body/eval_jaxpr/ppermute | solution.py:10
  196.4 12.2 %copy-start.14 = (f32[384,4]{0,1:T(4,128)}, f32[384,4]{0,1:T(4,128)S(1)}, u32[]{:S(2)}) copy-start(f32[384,4]{0,1:T(4,128)S(1)} %get-tuple-element.1185) | copy-start | bytes 18436 | tf_op jit(solution)/shard_map/while
  196.4 12.2 %copy-start.16 = (f32[384,4]{0,1:T(4,128)}, f32[384,4]{0,1:T(4,128)S(1)}, u32[]{:S(2)}) copy-start(f32[384,4]{0,1:T(4,128)S(1)} %get-tuple-element.1187) | copy-start | bytes 18436 | tf_op jit(solution)/shard_map/while
  196.4 35.0 %collective-permute-start = (bf16[384,128]{1,0:T(8,128)(2,1)}, bf16[384,128]{1,0:T(8,128)(2,1)}, u32[]{:S(2)}, u32[]{:S(2)}) collective-permute-start(bf16[384,128]{1,0:T(8,128)(2,1)} %get-tuple-element.1154), channel_id=1, source_target_pairs={{0,1},{1,2},{2,3},{3,4},{4,5},{5,6},{6,7},{7,0},{8,9},{9,10},{10,1... | collective-permute-start | bytes 294920 | tf_op jit(solution)/shard_map/while/body/eval_jaxpr/ppermute | solution.py:10
  196.4 35.8 %collective-permute-start.2 = (bf16[384,128]{1,0:T(8,128)(2,1)}, bf16[384,128]{1,0:T(8,128)(2,1)}, u32[]{:S(2)}, u32[]{:S(2)}) collective-permute-start(bf16[384,128]{1,0:T(8,128)(2,1)} %get-tuple-element.1155), channel_id=1, source_target_pairs={{0,1},{1,2},{2,3},{3,4},{4,5},{5,6},{6,7},{7,0},{8,9},{9,10},{10,1... | collective-permute-start | bytes 294920 | tf_op jit(solution)/shard_map/while/body/eval_jaxpr/ppermute | solution.py:10
  216.0 29.8 %collective-permute-start.6 = (f32[384,128]{1,0:T(8,128)}, f32[384,128]{1,0:T(8,128)}, u32[]{:S(2)}, u32[]{:S(2)}) collective-permute-start(f32[384,128]{1,0:T(8,128)} %maximum_add_fusion.11), channel_id=1, source_target_pairs={{0,1},{1,2},{2,3},{3,4},{4,5},{5,6},{6,7},{7,0},{8,9},{9,10},{10,1... | collective-permute-start | bytes 589832 | tf_op jit(solution)/shard_map/while/body/eval_jaxpr/ppermute | solution.py:10
  221.5 25.5 %collective-permute-start.4 = (f32[384,128]{1,0:T(8,128)}, f32[384,128]{1,0:T(8,128)}, u32[]{:S(2)}, u32[]{:S(2)}) collective-permute-start(f32[384,128]{1,0:T(8,128)} %maximum_add_fusion.9), channel_id=1, source_target_pairs={{0,1},{1,2},{2,3},{3,4},{4,5},{5,6},{6,7},{7,0},{8,9},{9,10},{10,1... | collective-permute-start | bytes 589832 | tf_op jit(solution)/shard_map/while/body/eval_jaxpr/ppermute | solution.py:10
  236.9 12.5 %collective-permute-start.1 = (bf16[384,128]{1,0:T(8,128)(2,1)}, bf16[384,128]{1,0:T(8,128)(2,1)}, u32[]{:S(2)}, u32[]{:S(2)}) collective-permute-start(bf16[384,128]{1,0:T(8,128)(2,1)} %collective-permute-done), channel_id=1, source_target_pairs={{0,1},{1,2},{2,3},{3,4},{4,5},{5,6},{6,7},{7,0},{8,9},{9,10},{10,1... | collective-permute-start | bytes 294920 | tf_op jit(solution)/shard_map/while/body/eval_jaxpr/ppermute | solution.py:10
  243.2 8.7 %collective-permute-start.3 = (bf16[384,128]{1,0:T(8,128)(2,1)}, bf16[384,128]{1,0:T(8,128)(2,1)}, u32[]{:S(2)}, u32[]{:S(2)}) collective-permute-start(bf16[384,128]{1,0:T(8,128)(2,1)} %collective-permute-done.2), channel_id=1, source_target_pairs={{0,1},{1,2},{2,3},{3,4},{4,5},{5,6},{6,7},{7,0},{8,9},{9,10},{10,1... | collective-permute-start | bytes 294920 | tf_op jit(solution)/shard_map/while/body/eval_jaxpr/ppermute | solution.py:10
  246.8 8.5 %collective-permute-start.7 = (f32[384,128]{1,0:T(8,128)S(1)}, f32[384,128]{1,0:T(8,128)}, u32[]{:S(2)}, u32[]{:S(2)}) collective-permute-start(f32[384,128]{1,0:T(8,128)S(1)} %maximum_add_fusion.12), channel_id=1, source_target_pairs={{0,1},{1,2},{2,3},{3,4},{4,5},{5,6},{6,7},{7,0},{8,9},{9,10},{10,1... | collective-permute-start | bytes 589832 | tf_op jit(solution)/shard_map/while/body/eval_jaxpr/ppermute | solution.py:10
  247.9 9.6 %collective-permute-start.5 = (f32[384,128]{1,0:T(8,128)S(1)}, f32[384,128]{1,0:T(8,128)}, u32[]{:S(2)}, u32[]{:S(2)}) collective-permute-start(f32[384,128]{1,0:T(8,128)S(1)} %maximum_add_fusion.10), channel_id=1, source_target_pairs={{0,1},{1,2},{2,3},{3,4},{4,5},{5,6},{6,7},{7,0},{8,9},{9,10},{10,1... | collective-permute-start | bytes 589832 | tf_op jit(solution)/shard_map/while/body/eval_jaxpr/ppermute | solution.py:10
  258.1 12.9 %copy-start.14 = (f32[384,4]{0,1:T(4,128)}, f32[384,4]{0,1:T(4,128)S(1)}, u32[]{:S(2)}) copy-start(f32[384,4]{0,1:T(4,128)S(1)} %get-tuple-element.1185) | copy-start | bytes 18436 | tf_op jit(solution)/shard_map/while
  258.1 12.9 %copy-start.16 = (f32[384,4]{0,1:T(4,128)}, f32[384,4]{0,1:T(4,128)S(1)}, u32[]{:S(2)}) copy-start(f32[384,4]{0,1:T(4,128)S(1)} %get-tuple-element.1187) | copy-start | bytes 18436 | tf_op jit(solution)/shard_map/while
  258.1 33.7 %collective-permute-start = (bf16[384,128]{1,0:T(8,128)(2,1)}, bf16[384,128]{1,0:T(8,128)(2,1)}, u32[]{:S(2)}, u32[]{:S(2)}) collective-permute-start(bf16[384,128]{1,0:T(8,128)(2,1)} %get-tuple-element.1154), channel_id=1, source_target_pairs={{0,1},{1,2},{2,3},{3,4},{4,5},{5,6},{6,7},{7,0},{8,9},{9,10},{10,1... | collective-permute-start | bytes 294920 | tf_op jit(solution)/shard_map/while/body/eval_jaxpr/ppermute | solution.py:10
  258.2 34.5 %collective-permute-start.2 = (bf16[384,128]{1,0:T(8,128)(2,1)}, bf16[384,128]{1,0:T(8,128)(2,1)}, u32[]{:S(2)}, u32[]{:S(2)}) collective-permute-start(bf16[384,128]{1,0:T(8,128)(2,1)} %get-tuple-element.1155), channel_id=1, source_target_pairs={{0,1},{1,2},{2,3},{3,4},{4,5},{5,6},{6,7},{7,0},{8,9},{9,10},{10,1... | collective-permute-start | bytes 294920 | tf_op jit(solution)/shard_map/while/body/eval_jaxpr/ppermute | solution.py:10
  277.1 27.5 %collective-permute-start.6 = (f32[384,128]{1,0:T(8,128)}, f32[384,128]{1,0:T(8,128)}, u32[]{:S(2)}, u32[]{:S(2)}) collective-permute-start(f32[384,128]{1,0:T(8,128)} %maximum_add_fusion.11), channel_id=1, source_target_pairs={{0,1},{1,2},{2,3},{3,4},{4,5},{5,6},{6,7},{7,0},{8,9},{9,10},{10,1... | collective-permute-start | bytes 589832 | tf_op jit(solution)/shard_map/while/body/eval_jaxpr/ppermute | solution.py:10
  281.1 24.6 %collective-permute-start.4 = (f32[384,128]{1,0:T(8,128)}, f32[384,128]{1,0:T(8,128)}, u32[]{:S(2)}, u32[]{:S(2)}) collective-permute-start(f32[384,128]{1,0:T(8,128)} %maximum_add_fusion.9), channel_id=1, source_target_pairs={{0,1},{1,2},{2,3},{3,4},{4,5},{5,6},{6,7},{7,0},{8,9},{9,10},{10,1... | collective-permute-start | bytes 589832 | tf_op jit(solution)/shard_map/while/body/eval_jaxpr/ppermute | solution.py:10
  297.3 16.6 %collective-permute-start.1 = (bf16[384,128]{1,0:T(8,128)(2,1)}, bf16[384,128]{1,0:T(8,128)(2,1)}, u32[]{:S(2)}, u32[]{:S(2)}) collective-permute-start(bf16[384,128]{1,0:T(8,128)(2,1)} %collective-permute-done), channel_id=1, source_target_pairs={{0,1},{1,2},{2,3},{3,4},{4,5},{5,6},{6,7},{7,0},{8,9},{9,10},{10,1... | collective-permute-start | bytes 294920 | tf_op jit(solution)/shard_map/while/body/eval_jaxpr/ppermute | solution.py:10
  304.5 9.4 %collective-permute-start.3 = (bf16[384,128]{1,0:T(8,128)(2,1)}, bf16[384,128]{1,0:T(8,128)(2,1)}, u32[]{:S(2)}, u32[]{:S(2)}) collective-permute-start(bf16[384,128]{1,0:T(8,128)(2,1)} %collective-permute-done.2), channel_id=1, source_target_pairs={{0,1},{1,2},{2,3},{3,4},{4,5},{5,6},{6,7},{7,0},{8,9},{9,10},{10,1... | collective-permute-start | bytes 294920 | tf_op jit(solution)/shard_map/while/body/eval_jaxpr/ppermute | solution.py:10
  305.6 8.7 %collective-permute-start.7 = (f32[384,128]{1,0:T(8,128)S(1)}, f32[384,128]{1,0:T(8,128)}, u32[]{:S(2)}, u32[]{:S(2)}) collective-permute-start(f32[384,128]{1,0:T(8,128)S(1)} %maximum_add_fusion.12), channel_id=1, source_target_pairs={{0,1},{1,2},{2,3},{3,4},{4,5},{5,6},{6,7},{7,0},{8,9},{9,10},{10,1... | collective-permute-start | bytes 589832 | tf_op jit(solution)/shard_map/while/body/eval_jaxpr/ppermute | solution.py:10
  306.6 10.0 %collective-permute-start.5 = (f32[384,128]{1,0:T(8,128)S(1)}, f32[384,128]{1,0:T(8,128)}, u32[]{:S(2)}, u32[]{:S(2)}) collective-permute-start(f32[384,128]{1,0:T(8,128)S(1)} %maximum_add_fusion.10), channel_id=1, source_target_pairs={{0,1},{1,2},{2,3},{3,4},{4,5},{5,6},{6,7},{7,0},{8,9},{9,10},{10,1... | collective-permute-start | bytes 589832 | tf_op jit(solution)/shard_map/while/body/eval_jaxpr/ppermute | solution.py:10
  318.9 41.5 %reduce-scatter.3.cloned.1.call-start = ((), (), s32[]{:S(2)}) async-start(), calls=%async_computation.9 | async-start | bytes 245760 | tf_op jit(solution)/shard_map/reduce_scatter | solution.py:145
  (71 other events, 149.7 us)
Sparse Core Ops, SparseCore 0:
  319.0 19.1 reduce-scatter.4
  340.6 19.7 reduce-scatter.2
where the time goes:
time: 371 us; the launch traced here: 369 us
  waiting for transfers between devices  80.3 us (22%)
  loops' own time  78.8 us (21%)
  starting transfers between devices  71.9 us (19%)
  local copies, waits for them, and re-layouts  56.9 us (15%)
  other arithmetic  30.3 us (8%)
  matrix products  18.3 us (5%)
  blocking collectives  17.9 us (5%)
  between operations  14.2 us (4%)
    another operation x1, loops' own time, local(): lax.fori_loop(0, cycle_size // 2, two_turns, (key_local, value_local) + s...  77.8 us
    ppermute x32, starting transfers between devices, passed_along(): return lax.ppermute(value, axis, pairs)  53.6 us
    ppermute x32, waiting for transfers between devices, passed_along(): return lax.ppermute(value, axis, pairs)  28.6 us
    while x152, local copies, waits for them, and re-layouts  24.6 us
    reduce_scatter x1, waiting for transfers between devices, local(): lax.psum_scatter(expanded_keys, 'head', scatter_dimension=0, tiled=True)  20.8 us
    add x8, other arithmetic, turn(): value_acc + value_part  10.4 us
    add x8, other arithmetic, turn(): key_acc + key_part  10.3 us
    all_to_all x1, blocking collectives, local(): lax.all_to_all(query_grad, 'head', split_axis=0, concat_axis=1, tiled=True)  9.84 us
  transfers between devices with their start and end apart: 39, of which 19 were waited for; matrix products, arithmetic and copies ran while one was open for 20% of the time, Pallas kernels for 0%

commit v1 on v0

v1 whole, which is shorter than its diff:
```python
import functools

import jax
import jax.numpy as jnp
from jax import lax
from jax.experimental import pallas as pl
from jax.experimental.pallas import tpu as pltpu
from jax.sharding import PartitionSpec as P

MESH = pl.DeviceIdType.MESH
LOG2E = 1.4426950408889634
BIG = 1e30


def dot(a, b, ca, cb):
    return lax.dot_general(a, b, (((ca,), (cb,)), ((), ())), preferred_element_type=jnp.float32)


def chunk_size(rows, keys):
    chunk = 512 if keys <= 512 else 128
    while rows % chunk:
        chunk //= 2
    return chunk


def kernel(nz, span_ref, q_ref, k_ref, v_ref, o_ref, do_ref, lse_ref, dq_ref, dk_ref, dv_ref,
           kv, pq, pdo, stats, pstats, kt, acc, acc0, dqt, dqt_p, dq_out, dq_in,
           part_out, part_in, line_out, line_in,
           x_send, x_recv, z_send, z_recv, p_send, p_recv, q_send, q_recv,
           r_send, r_recv, l_send, l_recv):
    f32, bf16 = jnp.float32, jnp.bfloat16
    t = k_ref.shape[0]
    head_size = k_ref.shape[1]
    rows = q_ref.shape[0]
    heads = rows // t
    keys = nz * t
    scale = head_size ** -0.5
    c = lax.axis_index("ctx")
    h = lax.axis_index("head")
    core = lax.rem(h, 2)
    x = lax.div(h, 2)
    y = lax.rem(c, 2)
    z = lax.div(c, 2)

    partner = {"ctx": c, "head": x * 2 + (1 - core)}

    def plane(q):
        xx = 1 - x if q % 2 else x
        yy = 1 - y if q // 2 else y
        return xx, yy

    def plane_id(q):
        xx, yy = plane(q)
        return {"ctx": z * 2 + yy, "head": xx * 2 + core}

    def line_id(d):
        return {"ctx": lax.rem(z + d, nz) * 2 + y, "head": h}

    barrier = pltpu.get_barrier_semaphore()
    peers = [partner] + [plane_id(q) for q in (1, 2, 3)] + [line_id(d) for d in range(1, nz)]
    for peer in peers:
        pl.semaphore_signal(barrier, inc=1, device_id=peer, device_id_type=MESH)

    kv[0, 0, 0] = k_ref[...]
    kv[0, 0, 1] = v_ref[...]

    prod = o_ref[...].astype(f32) * do_ref[...].astype(f32)
    prod_hi = prod.astype(bf16)
    prod_lo = (prod - prod_hi.astype(f32)).astype(bf16)
    ones = jnp.ones((8, head_size), bf16)
    delta = dot(ones, prod_hi, 1, 1) + dot(ones, prod_lo, 1, 1)
    stats[0:1, :] = lse_ref[...] * LOG2E
    stats[1:2, :] = delta[0:1, :]

    pl.semaphore_wait(barrier, len(peers))

    def remote(src, dst, ss, rs, dev):
        return pltpu.make_async_remote_copy(
            src_ref=src, dst_ref=dst, send_sem=ss, recv_sem=rs, device_id=dev, device_id_type=MESH)

    zc = [None] + [remote(kv.at[0, 0], kv.at[0, nz - d], z_send.at[d], z_recv.at[nz - d], line_id(d))
                   for d in range(1, nz)]
    pc = {(q, d): remote(kv.at[0, d], kv.at[q, d], p_send.at[q, d], p_recv.at[q, d], plane_id(q))
          for q in (1, 2, 3) for d in range(nz)}
    xc = [remote(q_ref, pq, x_send.at[0], x_recv.at[0], partner),
          remote(do_ref, pdo, x_send.at[1], x_recv.at[1], partner),
          remote(stats, pstats, x_send.at[2], x_recv.at[2], partner)]
    for d in range(1, nz):
        zc[d].start()
    for q in (1, 2, 3):
        pc[q, 0].start()
    xc[2].start()
    xc[0].start()
    xc[1].start()

    def z_arrival(d):
        return remote(kv.at[0, 0], kv.at[0, d], z_send.at[nz - d], z_recv.at[d], line_id(nz - d))

    for d in sorted(range(1, nz), key=lambda d: min(d, nz - d)):
        z_arrival(d).wait_recv()
        for q in (1, 2, 3):
            pc[q, d].start()

    own_span = c * (lax.axis_size("head") // 2) + x
    own_place = span_ref[own_span]
    chunk = chunk_size(rows, keys)

    def prepare(q):
        block = kv[q, :, 0].reshape(keys, head_size)
        kt[...] = block.astype(f32).T.astype(bf16)

    def work(q, row_q, row_do, row_stats, row_core, dq_acc, first, total, total_first):
        xx, yy = plane(q)
        lifts = []
        for d in range(nz):
            zz = lax.rem(z + d, nz)
            place = span_ref[(zz * 2 + yy) * (lax.axis_size("head") // 2) + xx]
            lifts.append(jnp.where(place > own_place, jnp.float32(BIG), jnp.float32(0.0)))
        if total_first:
            total[...] = jnp.zeros(total.shape, f32)

        def body(i, carry):
            low = pl.multiple_of(i * chunk, chunk)
            at = pl.ds(low, chunk)
            qs = row_q[at, :]
            gs = row_do[at, :]
            lse = row_stats[0:1, at]
            delt = row_stats[1:2, at]
            kb = kv[q, :, 0].reshape(keys, head_size)
            vb = kv[q, :, 1].reshape(keys, head_size)
            s = dot(kb, qs, 1, 1)
            dp = dot(vb, gs, 1, 1)
            ps, dss = [], []
            for d in range(nz):
                part = slice(d * t, (d + 1) * t)
                e = s[part] * (scale * LOG2E) - (lse + lifts[d])
                if q == 0 and d == 0:
                    key_at = lax.broadcasted_iota(jnp.int32, (t, chunk), 0) + core * t
                    row_at = lax.broadcasted_iota(jnp.int32, (t, chunk), 1) + low
                    row_at = lax.div(row_at, heads) + row_core * t
                    e = jnp.where(key_at <= row_at, e, -BIG)
                p = jnp.exp2(e)
                ps.append(p.astype(bf16))
                dss.append((p * (dp[part] - delt)).astype(bf16))
            p = jnp.concatenate(ps, axis=0)
            ds = jnp.concatenate(dss, axis=0)
            total[0] += dot(ds, qs, 1, 0)
            total[1] += dot(p, gs, 1, 0)
            dqt = dot(kt[...], ds, 1, 0)
            if first:
                dq_acc[:, at] = dqt
            else:
                dq_acc[:, at] += dqt
            return carry

        lax.fori_loop(0, rows // chunk, body, 0)

    for copy in xc:
        copy.wait_recv()
    prepare(0)
    work(0, pq, pdo, pstats, 1 - core, dqt_p, True, acc0, True)
    rc = {}
    for q in (1, 2, 3):
        for d in range(nz):
            pc[q, d].wait_recv()
        prepare(q)
        work(q, pq, pdo, pstats, 1 - core, dqt_p, False, acc, True)
        work(q, q_ref, do_ref, stats, core, dqt, q == 1, acc, False)
        for d in range(nz):
            part_out[q - 1, d] = acc[:, d * t:(d + 1) * t, :].astype(bf16)
        rc[q] = remote(part_out.at[q - 1], part_in.at[q - 1], r_send.at[q - 1], r_recv.at[q - 1], plane_id(q))
        rc[q].start()
    dq_out[...] = dqt_p[...].T.astype(bf16)
    qc = remote(dq_out, dq_in, q_send, q_recv, partner)
    qc.start()
    prepare(0)
    work(0, q_ref, do_ref, stats, core, dqt, False, acc0, False)
    for q in (1, 2, 3):
        rc[q].wait_recv()

    def plane_sum(d):
        value = acc0[:, d * t:(d + 1) * t, :]
        for q in (1, 2, 3):
            value = value + part_in[q - 1, d].astype(f32)
        return value

    lc = [None]
    for d in range(1, nz):
        line_out[d - 1] = plane_sum(d).astype(bf16)
        lc.append(remote(line_out.at[d - 1], line_in.at[nz - d - 1], l_send.at[d - 1],
                         l_recv.at[nz - d - 1], line_id(d)))
        lc[d].start()
    own = plane_sum(0)
    qc.wait_recv()
    dq_ref[...] = ((dqt[...].T + dq_in[...].astype(f32)) * scale).astype(bf16)
    for d in range(1, nz):
        remote(line_out.at[nz - d - 1], line_in.at[d - 1], l_send.at[nz - d - 1],
               l_recv.at[d - 1], line_id(nz - d)).wait_recv()
        own = own + line_in[d - 1].astype(f32)
    dk_ref[...] = (own[0] * scale).astype(bf16)
    dv_ref[...] = own[1].astype(bf16)

    for copy in xc + zc[1:] + list(pc.values()) + list(rc.values()) + [qc] + lc[1:]:
        copy.wait_send()


def local(query_rows, key_matrix, value_matrix, output_rows, out_grad, log_norm, span_order):
    f32, bf16 = jnp.float32, jnp.bfloat16
    t, heads, d = query_rows.shape
    nz = lax.axis_size("ctx") // 2
    rows = t * heads
    keys = nz * t
    flat = lambda a: a.reshape(-1, d)
    vm = pl.BlockSpec(memory_space=pltpu.VMEM)
    dma = lambda *s: pltpu.SemaphoreType.DMA(s)
    dq, dk, dv = pl.pallas_call(
        functools.partial(kernel, nz),
        out_shape=(jax.ShapeDtypeStruct((rows, d), bf16), jax.ShapeDtypeStruct((t, d), bf16),
                   jax.ShapeDtypeStruct((t, d), bf16)),
        in_specs=[pl.BlockSpec(memory_space=pltpu.SMEM)] + [vm] * 6,
        out_specs=(vm, vm, vm),
        scratch_shapes=[
            pltpu.VMEM((4, nz, 2, t, d), bf16),
            pltpu.VMEM((rows, d), bf16),
            pltpu.VMEM((rows, d), bf16),
            pltpu.VMEM((2, rows), f32),
            pltpu.VMEM((2, rows), f32),
            pltpu.VMEM((d, keys), bf16),
            pltpu.VMEM((2, keys, d), f32),
            pltpu.VMEM((2, keys, d), f32),
            pltpu.VMEM((d, rows), f32),
            pltpu.VMEM((d, rows), f32),
            pltpu.VMEM((rows, d), bf16),
            pltpu.VMEM((rows, d), bf16),
            pltpu.VMEM((3, nz, 2, t, d), bf16),
            pltpu.VMEM((3, nz, 2, t, d), bf16),
            pltpu.VMEM((nz - 1, 2, t, d), bf16),
            pltpu.VMEM((nz - 1, 2, t, d), bf16),
            dma(3), dma(3), dma(nz), dma(nz), dma(4, nz), dma(4, nz),
            pltpu.SemaphoreType.DMA, pltpu.SemaphoreType.DMA,
            dma(3), dma(3), dma(nz - 1), dma(nz - 1),
        ],
        compiler_params=pltpu.CompilerParams(
            collective_id=0, has_side_effects=True, vmem_limit_bytes=48 * 1024 * 1024),
    )(span_order, flat(query_rows), flat(key_matrix), flat(value_matrix), flat(output_rows),
      flat(out_grad), log_norm.reshape(1, rows))
    return dq.reshape(query_rows.shape), dk.reshape(key_matrix.shape), dv.reshape(value_matrix.shape)


def solution(mesh):
    three = P(("ctx", "head"), None, None)
    in_specs = (three, three, three, three, three, P(("ctx", "head"), None), P())
    out_specs = (three, three, three)
    return jax.shard_map(local, mesh=mesh, in_specs=in_specs, out_specs=out_specs, check_vma=False)
```

time: 371 us -> 48 us (0.13)
  waiting for transfers between devices: 80.3 us -> 0 us
  loops' own time: 78.8 us -> 0 us
  starting transfers between devices: 71.9 us -> 0 us
  local copies, waits for them, and re-layouts: 56.9 us -> 6.46 us
  Pallas kernels: 0 us -> 40.5 us
  other arithmetic: 30.3 us -> 0 us
  matrix products: 18.3 us -> 0 us
  blocking collectives: 17.9 us -> 0 us
  between operations: 14.2 us -> 0.68 us
    another operation x33 -> x0, loops' own time: 78.8 us -> none  [the longest x1 77.8 us: local(): lax.fori_loop(0, cycle_size // 2, two_turns, (key_local, value_local) + s...]
    ppermute x32 -> x0, starting transfers between devices: 53.6 us -> none  [passed_along(): return lax.ppermute(value, axis, pairs)]
    pallas_call x0 -> x1, Pallas kernels: none -> 40.5 us  [local(): pl.pallas_call(functools.partial(kernel, nz), out_shape=(jax.ShapeDtypeSt...]
    ppermute x32 -> x0, waiting for transfers between devices: 28.6 us -> none  [passed_along(): return lax.ppermute(value, axis, pairs)]
    reduce_scatter x2 -> x0, waiting for transfers between devices: 27.3 us -> none  [the longest x1 20.8 us: local(): lax.psum_scatter(expanded_keys, 'head', scatter_dimension=0, tiled=True)]
    while x152 -> x0, local copies, waits for them, and re-layouts: 24.6 us -> none
    all_to_all x5 -> x0, waiting for transfers between devices: 24.4 us -> none  [the longest x1 6.55 us: local(): lax.all_to_all(output_rows, 'head', split_axis=1, concat_axis=0, tiled=True)]
    add x68 -> x0, other arithmetic: 23.8 us -> none  [the longest x8 10.4 us: turn(): value_acc + value_part]
  transfers between devices with their start and end apart: 39 -> 0, of which waited for: 19 -> 0; matrix products, arithmetic and copies ran while one was open for 20% -> 0% of each run, Pallas kernels for 0% -> 0%
where the time goes in v1:
time: 48 us; the launch traced here: 47.7 us
  Pallas kernels  40.5 us (84%)
  local copies, waits for them, and re-layouts  6.46 us (13%)
  between operations  0.68 us (1%)
    pallas_call x1, Pallas kernels, local(): pl.pallas_call(functools.partial(kernel, nz), out_shape=(jax.ShapeDtypeSt...  40.5 us
    unnamed x18, local copies, waits for them, and re-layouts  6.38 us

profile of v1, /device:TPU:0, one launch (start us, length us, event | category | flops | bytes accessed | tf_op | source)
XLA Modules:
  0.0 47.7 jit_solution(10694337647054124511)
XLA Ops:
  0.6 0.0 copy-start.6
  0.6 0.7 %copy-done.6 = f32[96,16]{0,1:T(8,128)S(1)} copy-done((f32[96,16]{0,1:T(8,128)S(1)}, f32[96,16]{0,1:T(8,128)}, u32[]{:S(2)}) %copy-start.6) | copy-done | bytes 6168
  1.3 0.1 copy.11
  1.4 0.0 copy-start.3
  1.4 0.0 copy-start.4
  1.4 0.0 copy-start.5
  1.4 0.1 reshape.38.lse_ref
  1.5 0.6 %copy-done.3 = bf16[96,1,128]{2,0,1:T(8,128)(2,1)S(1)} copy-done((bf16[96,1,128]{2,0,1:T(8,128)(2,1)S(1)}, bf16[96,1,128]{2,0,1:T(8,128)(2,1)}, u32[]{:S(2)}) %copy-start.3) | copy-done | bytes 24600
  2.2 0.0 copy-done.4
  2.2 0.0 copy-done.5
  2.2 0.0 copy-start
  2.2 1.0 %copy-done = bf16[96,16,128]{2,1,0:T(8,128)(2,1)S(1)} copy-done((bf16[96,16,128]{2,1,0:T(8,128)(2,1)S(1)}, bf16[96,16,128]{2,1,0:T(8,128)(2,1)}, u32[]{:S(2)}) %copy-start) | copy-done | bytes 393240
  3.2 0.0 copy-start.1
  3.2 1.0 %copy-done.1 = bf16[96,16,128]{2,1,0:T(8,128)(2,1)S(1)} copy-done((bf16[96,16,128]{2,1,0:T(8,128)(2,1)S(1)}, bf16[96,16,128]{2,1,0:T(8,128)(2,1)}, u32[]{:S(2)}) %copy-start.1) | copy-done | bytes 393240
  4.2 0.0 copy-start.2
  4.2 1.0 %copy-done.2 = bf16[96,16,128]{2,1,0:T(8,128)(2,1)S(1)} copy-done((bf16[96,16,128]{2,1,0:T(8,128)(2,1)S(1)}, bf16[96,16,128]{2,1,0:T(8,128)(2,1)}, u32[]{:S(2)}) %copy-start.2) | copy-done | bytes 393240
  5.2 40.5 %shard_map.94 = (bf16[1536,128]{1,0:T(8,128)(2,1)S(1)}, bf16[96,128]{1,0:T(8,128)(2,1)S(1)}, bf16[96,128]{1,0:T(8,128)(2,1)S(1)}) custom-call(s32[16]{0:T(128)S(1)} %copy-done.5, bf16[1536,128]{1,0:T(8,128)(2,1)S(1)} %bitcast.9, bf16[96,128]{1,0:T(8,128)(2,1)S(1)} %bitcast.14, bf16[96,128]{1,0:T(8,128)(2,1)S(1)} %bitcast.15, bf16[1536,128]{1,0:T(8,128)(2,1)S(1)} %bitcast.10, ...), custom_call_target="tpu_custom_call" | custom-call | tf_op jit(solution)/shard_map/pallas_call | solution.py:216
  45.7 0.7 %copy.15 = bf16[96,16,128]{2,1,0:T(8,128)(2,1)} copy(bf16[96,16,128]{2,1,0:T(8,128)(2,1)S(1)} %bitcast.8) | data formatting | bytes 786432
  46.5 0.6 %copy.16 = bf16[96,1,128]{2,0,1:T(8,128)(2,1)} copy(bf16[96,1,128]{2,0,1:T(8,128)(2,1)S(1)} %bitcast.13) | data formatting | bytes 49152
  47.1 0.6 %copy.17 = bf16[96,1,128]{2,0,1:T(8,128)(2,1)} copy(bf16[96,1,128]{2,0,1:T(8,128)(2,1)S(1)} %bitcast.12) | data formatting | bytes 49152
Async XLA Ops:
  0.6 0.7 %copy-start.6 = (f32[96,16]{0,1:T(8,128)S(1)}, f32[96,16]{0,1:T(8,128)}, u32[]{:S(2)}) copy-start(f32[96,16]{0,1:T(8,128)} %param.12) | copy-start | bytes 18436
  1.4 0.7 %copy-start.3 = (bf16[96,1,128]{2,0,1:T(8,128)(2,1)S(1)}, bf16[96,1,128]{2,0,1:T(8,128)(2,1)}, u32[]{:S(2)}) copy-start(bf16[96,1,128]{2,0,1:T(8,128)(2,1)} %param.8) | copy-start | bytes 73732
  1.4 0.7 %copy-start.4 = (bf16[96,1,128]{2,0,1:T(8,128)(2,1)S(1)}, bf16[96,1,128]{2,0,1:T(8,128)(2,1)}, u32[]{:S(2)}) copy-start(bf16[96,1,128]{2,0,1:T(8,128)(2,1)} %param.9) | copy-start | bytes 73732
  1.4 0.7 %copy-start.5 = (s32[16]{0:T(128)S(1)}, s32[16]{0:T(128)}, u32[]{:S(2)}) copy-start(s32[16]{0:T(128)} %span_ref.1) | copy-start | bytes 196
  2.2 1.0 %copy-start = (bf16[96,16,128]{2,1,0:T(8,128)(2,1)S(1)}, bf16[96,16,128]{2,1,0:T(8,128)(2,1)}, u32[]{:S(2)}) copy-start(bf16[96,16,128]{2,1,0:T(8,128)(2,1)} %param.7) | copy-start | bytes 1179652
  3.2 1.0 %copy-start.1 = (bf16[96,16,128]{2,1,0:T(8,128)(2,1)S(1)}, bf16[96,16,128]{2,1,0:T(8,128)(2,1)}, u32[]{:S(2)}) copy-start(bf16[96,16,128]{2,1,0:T(8,128)(2,1)} %param.10) | copy-start | bytes 1179652
  4.2 1.0 %copy-start.2 = (bf16[96,16,128]{2,1,0:T(8,128)(2,1)S(1)}, bf16[96,16,128]{2,1,0:T(8,128)(2,1)}, u32[]{:S(2)}) copy-start(bf16[96,16,128]{2,1,0:T(8,128)(2,1)} %param.11) | copy-start | bytes 1179652

commit v2 on v1

--- a/solution.py
+++ b/solution.py
@@ -17,14 +17,14 @@
 
 
 def chunk_size(rows, keys):
-    chunk = 512 if keys <= 512 else 128
+    chunk = 1536 if keys <= 512 else 128
     while rows % chunk:
         chunk //= 2
     return chunk
 
 
-def kernel(nz, span_ref, q_ref, k_ref, v_ref, o_ref, do_ref, lse_ref, dq_ref, dk_ref, dv_ref,
-           kv, pq, pdo, stats, pstats, kt, acc, acc0, dqt, dqt_p, dq_out, dq_in,
+def kernel(nz, span_ref, q_hbm, k_ref, v_ref, o_hbm, do_hbm, lse_hbm, dq_ref, dk_ref, dv_ref,
+           q_ref, o_ref, do_ref, lse_ref, in_sem, kv, pq, pdo, stats, pstats, kt, acc, acc0, dqt, dqt_p, dq_out, dq_in,
            part_out, part_in, line_out, line_in,
            x_send, x_recv, z_send, z_recv, p_send, p_recv, q_send, q_recv,
            r_send, r_recv, l_send, l_recv):
@@ -56,49 +56,72 @@
     def line_id(d):
         return {"ctx": lax.rem(z + d, nz) * 2 + y, "head": h}
 
+    loads = [pltpu.make_async_copy(src, dst, in_sem.at[i]) for i, (src, dst) in enumerate((
+        (k_ref, kv.at[0, 0, 0]), (v_ref, kv.at[0, 0, 1]), (do_hbm, do_ref), (o_hbm, o_ref),
+        (lse_hbm, lse_ref), (q_hbm, q_ref)))]
+    for load in loads:
+        load.start()
     barrier = pltpu.get_barrier_semaphore()
     peers = [partner] + [plane_id(q) for q in (1, 2, 3)] + [line_id(d) for d in range(1, nz)]
     for peer in peers:
         pl.semaphore_signal(barrier, inc=1, device_id=peer, device_id_type=MESH)
 
-    kv[0, 0, 0] = k_ref[...]
-    kv[0, 0, 1] = v_ref[...]
-
+    loads[0].wait()
+    loads[1].wait()
+    pl.semaphore_wait(barrier, len(peers))
+
+    def remote(src, dst, ss, rs, dev):
+        return pltpu.make_async_remote_copy(
+            src_ref=src, dst_ref=dst, send_sem=ss, recv_sem=rs, device_id=dev, device_id_type=MESH)
+
+    zc = [None] + [remote(kv.at[0, 0], kv.at[0, nz - d], z_send.at[d], z_recv.at[nz - d], line_id(d))
+                   for d in range(1, nz)]
+    pc = {(q, d): remote(kv.at[0, d], kv.at[q, d], p_send.at[q, d], p_recv.at[q, d], plane_id(q))
+          for q in (1, 2) for d in range(nz)}
+    for d in range(nz):
+        for half in range(2):
+            pc[3 + half, d] = remote(
+                kv.at[1 + half, d, half], kv.at[3, d, half], p_send.at[3 + half, d],
+                p_recv.at[3 + half, d], plane_id(2 - half))
+    xc = [remote(q_hbm, pq, x_send.at[0], x_recv.at[0], partner),
+          remote(do_hbm, pdo, x_send.at[1], x_recv.at[1], partner),
+          remote(stats, pstats, x_send.at[2], x_recv.at[2], partner)]
+    for d in range(1, nz):
+        zc[d].start()
+    for q in (1, 2):
+        pc[q, 0].start()
+    xc[0].start()
+    xc[1].start()
+    loads[2].wait()
+    loads[3].wait()
     prod = o_ref[...].astype(f32) * do_ref[...].astype(f32)
     prod_hi = prod.astype(bf16)
     prod_lo = (prod - prod_hi.astype(f32)).astype(bf16)
     ones = jnp.ones((8, head_size), bf16)
     delta = dot(ones, prod_hi, 1, 1) + dot(ones, prod_lo, 1, 1)
-    stats[0:1, :] = lse_ref[...] * LOG2E
+    loads[4].wait()
+    rest = lse_ref[...]
+    pick = (lax.div(lax.broadcasted_iota(jnp.int32, (t, rows), 1), heads)
+            == lax.broadcasted_iota(jnp.int32, (t, rows), 0)).astype(f32).astype(bf16)
+    spread = jnp.zeros((heads, rows), f32)
+    for _ in range(3):
+        piece = rest.astype(bf16)
+        rest = rest - piece.astype(f32)
+        spread = spread + dot(piece, pick, 1, 0)
+    mine = (lax.rem(lax.broadcasted_iota(jnp.int32, (heads, rows), 1), heads)
+            == lax.broadcasted_iota(jnp.int32, (heads, rows), 0))
+    stats[0:1, :] = jnp.sum(jnp.where(mine, spread, 0.0), axis=0, keepdims=True) * LOG2E
     stats[1:2, :] = delta[0:1, :]
-
-    pl.semaphore_wait(barrier, len(peers))
-
-    def remote(src, dst, ss, rs, dev):
-        return pltpu.make_async_remote_copy(
-            src_ref=src, dst_ref=dst, send_sem=ss, recv_sem=rs, device_id=dev, device_id_type=MESH)
-
-    zc = [None] + [remote(kv.at[0, 0], kv.at[0, nz - d], z_send.at[d], z_recv.at[nz - d], line_id(d))
-                   for d in range(1, nz)]
-    pc = {(q, d): remote(kv.at[0, d], kv.at[q, d], p_send.at[q, d], p_recv.at[q, d], plane_id(q))
-          for q in (1, 2, 3) for d in range(nz)}
-    xc = [remote(q_ref, pq, x_send.at[0], x_recv.at[0], partner),
-          remote(do_ref, pdo, x_send.at[1], x_recv.at[1], partner),
-          remote(stats, pstats, x_send.at[2], x_recv.at[2], partner)]
-    for d in range(1, nz):
-        zc[d].start()
-    for q in (1, 2, 3):
-        pc[q, 0].start()
     xc[2].start()
-    xc[0].start()
-    xc[1].start()
+    loads[5].wait()
+
 
     def z_arrival(d):
         return remote(kv.at[0, 0], kv.at[0, d], z_send.at[nz - d], z_recv.at[d], line_id(nz - d))
 
     for d in sorted(range(1, nz), key=lambda d: min(d, nz - d)):
         z_arrival(d).wait_recv()
-        for q in (1, 2, 3):
+        for q in (1, 2):
             pc[q, d].start()
 
     own_span = c * (lax.axis_size("head") // 2) + x
@@ -159,10 +182,16 @@
         copy.wait_recv()
     prepare(0)
     work(0, pq, pdo, pstats, 1 - core, dqt_p, True, acc0, True)
+    for d in [0] + sorted(range(1, nz), key=lambda d: min(d, nz - d)):
+        for q in (1, 2):
+            pc[q, d].wait_recv()
+            pc[q + 2, d].start()
     rc = {}
     for q in (1, 2, 3):
-        for d in range(nz):
-            pc[q, d].wait_recv()
+        if q == 3:
+            for d in range(nz):
+                pc[3, d].wait_recv()
+                pc[4, d].wait_recv()
         prepare(q)
         work(q, pq, pdo, pstats, 1 - core, dqt_p, False, acc, True)
         work(q, q_ref, do_ref, stats, core, dqt, q == 1, acc, False)
@@ -212,14 +241,20 @@
     keys = nz * t
     flat = lambda a: a.reshape(-1, d)
     vm = pl.BlockSpec(memory_space=pltpu.VMEM)
+    hbm = pl.BlockSpec(memory_space=pltpu.HBM)
     dma = lambda *s: pltpu.SemaphoreType.DMA(s)
     dq, dk, dv = pl.pallas_call(
         functools.partial(kernel, nz),
         out_shape=(jax.ShapeDtypeStruct((rows, d), bf16), jax.ShapeDtypeStruct((t, d), bf16),
                    jax.ShapeDtypeStruct((t, d), bf16)),
-        in_specs=[pl.BlockSpec(memory_space=pltpu.SMEM)] + [vm] * 6,
+        in_specs=[pl.BlockSpec(memory_space=pltpu.SMEM)] + [hbm] * 6,
         out_specs=(vm, vm, vm),
         scratch_shapes=[
+            pltpu.VMEM((rows, d), bf16),
+            pltpu.VMEM((rows, d), bf16),
+            pltpu.VMEM((rows, d), bf16),
+            pltpu.VMEM((heads, t), f32),
+            dma(6),
             pltpu.VMEM((4, nz, 2, t, d), bf16),
             pltpu.VMEM((rows, d), bf16),
             pltpu.VMEM((rows, d), bf16),
@@ -236,14 +271,14 @@
             pltpu.VMEM((3, nz, 2, t, d), bf16),
             pltpu.VMEM((nz - 1, 2, t, d), bf16),
             pltpu.VMEM((nz - 1, 2, t, d), bf16),
-            dma(3), dma(3), dma(nz), dma(nz), dma(4, nz), dma(4, nz),
+            dma(3), dma(3), dma(nz), dma(nz), dma(5, nz), dma(5, nz),
             pltpu.SemaphoreType.DMA, pltpu.SemaphoreType.DMA,
             dma(3), dma(3), dma(nz - 1), dma(nz - 1),
         ],
         compiler_params=pltpu.CompilerParams(
-            collective_id=0, has_side_effects=True, vmem_limit_bytes=48 * 1024 * 1024),
+            collective_id=0, has_side_effects=True, vmem_limit_bytes=63 * 1024 * 1024 + 512 * 1024),
     )(span_order, flat(query_rows), flat(key_matrix), flat(value_matrix), flat(output_rows),
-      flat(out_grad), log_norm.reshape(1, rows))
+      flat(out_grad), log_norm.T)
     return dq.reshape(query_rows.shape), dk.reshape(key_matrix.shape), dv.reshape(value_matrix.shape)
 
 

time: 48 us -> 40.5 us (0.84)
  Pallas kernels: 40.5 us -> 36.5 us
  local copies, waits for them, and re-layouts: 6.46 us -> 3.13 us
    pallas_call x1, Pallas kernels: 40.5 us -> 36.5 us  [local(): pl.pallas_call(functools.partial(kernel, nz), out_shape=(jax.ShapeDtypeSt...]
    unnamed x18 -> x7, local copies, waits for them, and re-layouts: 6.38 us -> 3.13 us
where the time goes in v2:
time: 40.5 us; the launch traced here: 40.3 us
  Pallas kernels  36.5 us (90%)
  local copies, waits for them, and re-layouts  3.13 us (8%)
  between operations  0.65 us (2%)
    pallas_call x1, Pallas kernels, local(): pl.pallas_call(functools.partial(kernel, nz), out_shape=(jax.ShapeDtypeSt...  36.5 us
    unnamed x7, local copies, waits for them, and re-layouts  3.13 us

profile of v2, /device:TPU:0, one launch (start us, length us, event | category | flops | bytes accessed | tf_op | source)
XLA Modules:
  0.0 40.3 jit_solution(4864619314270991855)
XLA Ops:
  0.6 36.5 %shard_map.94 = (bf16[1536,128]{1,0:T(8,128)(2,1)}, bf16[96,128]{1,0:T(8,128)(2,1)}, bf16[96,128]{1,0:T(8,128)(2,1)}) custom-call(s32[16]{0:T(128)} %span_ref.1, bf16[1536,128]{1,0:T(8,128)(2,1)} %bitcast.10, bf16[96,128]{1,0:T(8,128)(2,1)} %bitcast.15, bf16[96,128]{1,0:T(8,128)(2,1)} %bitcast.16, bf16[1536,128]{1,0:T(8,128)(2,1)} %bitcast.11, ...), custom_call_target="tpu_custom_call" | custom-call | tf_op jit(solution)/shard_map/pallas_call | solution.py:246
  37.2 0.0 copy-start.1
  37.2 1.8 %copy.13 = bf16[96,16,128]{2,1,0:T(8,128)(2,1)} copy(bf16[96,16,128]{2,1,0:T(8,128)(2,1)} %bitcast.9) | data formatting | bytes 786432
  39.0 0.0 copy-done.1
  39.0 0.0 copy-start
  39.0 0.6 %copy.14 = bf16[96,1,128]{2,0,1:T(8,128)(2,1)} copy(bf16[96,1,128]{2,0,1:T(8,128)(2,1)S(1)} %bitcast.14) | data formatting | bytes 49152
  39.6 0.1 copy-done
  39.7 0.6 %copy.15 = bf16[96,1,128]{2,0,1:T(8,128)(2,1)} copy(bf16[96,1,128]{2,0,1:T(8,128)(2,1)S(1)} %bitcast.13) | data formatting | bytes 49152
Async XLA Ops:
  37.2 1.8 %copy-start.1 = (bf16[96,128]{1,0:T(8,128)(2,1)S(1)}, bf16[96,128]{1,0:T(8,128)(2,1)}, u32[]{:S(2)}) copy-start(bf16[96,128]{1,0:T(8,128)(2,1)} %get-tuple-element.7) | copy-start | bytes 73732
  39.0 0.7 %copy-start = (bf16[96,128]{1,0:T(8,128)(2,1)S(1)}, bf16[96,128]{1,0:T(8,128)(2,1)}, u32[]{:S(2)}) copy-start(bf16[96,128]{1,0:T(8,128)(2,1)} %get-tuple-element.8) | copy-start | bytes 73732

commit v3 on v2

--- a/solution.py
+++ b/solution.py
@@ -187,6 +187,7 @@
             pc[q, d].wait_recv()
             pc[q + 2, d].start()
     rc = {}
+    far_first = sorted(range(nz), key=lambda d: -min(d, nz - d))
     for q in (1, 2, 3):
         if q == 3:
             for d in range(nz):
@@ -195,29 +196,29 @@
         prepare(q)
         work(q, pq, pdo, pstats, 1 - core, dqt_p, False, acc, True)
         work(q, q_ref, do_ref, stats, core, dqt, q == 1, acc, False)
-        for d in range(nz):
+        for d in far_first:
             part_out[q - 1, d] = acc[:, d * t:(d + 1) * t, :].astype(bf16)
-        rc[q] = remote(part_out.at[q - 1], part_in.at[q - 1], r_send.at[q - 1], r_recv.at[q - 1], plane_id(q))
-        rc[q].start()
+            rc[q, d] = remote(part_out.at[q - 1, d], part_in.at[q - 1, d], r_send.at[q - 1, d],
+                              r_recv.at[q - 1, d], plane_id(q))
+            rc[q, d].start()
     dq_out[...] = dqt_p[...].T.astype(bf16)
     qc = remote(dq_out, dq_in, q_send, q_recv, partner)
     qc.start()
     prepare(0)
     work(0, q_ref, do_ref, stats, core, dqt, False, acc0, False)
-    for q in (1, 2, 3):
-        rc[q].wait_recv()
 
     def plane_sum(d):
         value = acc0[:, d * t:(d + 1) * t, :]
         for q in (1, 2, 3):
+            rc[q, d].wait_recv()
             value = value + part_in[q - 1, d].astype(f32)
         return value
 
-    lc = [None]
-    for d in range(1, nz):
+    lc = {}
+    for d in far_first[:-1]:
         line_out[d - 1] = plane_sum(d).astype(bf16)
-        lc.append(remote(line_out.at[d - 1], line_in.at[nz - d - 1], l_send.at[d - 1],
-                         l_recv.at[nz - d - 1], line_id(d)))
+        lc[d] = remote(line_out.at[d - 1], line_in.at[nz - d - 1], l_send.at[d - 1],
+                       l_recv.at[nz - d - 1], line_id(d))
         lc[d].start()
     own = plane_sum(0)
     qc.wait_recv()
@@ -229,7 +230,7 @@
     dk_ref[...] = (own[0] * scale).astype(bf16)
     dv_ref[...] = own[1].astype(bf16)
 
-    for copy in xc + zc[1:] + list(pc.values()) + list(rc.values()) + [qc] + lc[1:]:
+    for copy in xc + zc[1:] + list(pc.values()) + list(rc.values()) + [qc] + list(lc.values()):
         copy.wait_send()
 
 
@@ -273,7 +274,7 @@
             pltpu.VMEM((nz - 1, 2, t, d), bf16),
             dma(3), dma(3), dma(nz), dma(nz), dma(5, nz), dma(5, nz),
             pltpu.SemaphoreType.DMA, pltpu.SemaphoreType.DMA,
-            dma(3), dma(3), dma(nz - 1), dma(nz - 1),
+            dma(3, nz), dma(3, nz), dma(nz - 1), dma(nz - 1),
         ],
         compiler_params=pltpu.CompilerParams(
             collective_id=0, has_side_effects=True, vmem_limit_bytes=63 * 1024 * 1024 + 512 * 1024),

time: 40.5 us -> 39.6 us (0.978)
  Pallas kernels: 36.5 us -> 35.6 us
    pallas_call x1, Pallas kernels: 36.5 us -> 35.6 us  [local(): pl.pallas_call(functools.partial(kernel, nz), out_shape=(jax.ShapeDtypeSt...]
where the time goes in v3:
time: 39.6 us; the launch traced here: 39.4 us
  Pallas kernels  35.6 us (90%)
  local copies, waits for them, and re-layouts  3.13 us (8%)
  between operations  0.65 us (2%)
    pallas_call x1, Pallas kernels, local(): pl.pallas_call(functools.partial(kernel, nz), out_shape=(jax.ShapeDtypeSt...  35.6 us
    unnamed x7, local copies, waits for them, and re-layouts  3.13 us

profile of v3, /device:TPU:0, one launch (start us, length us, event | category | flops | bytes accessed | tf_op | source)
XLA Modules:
  0.0 39.4 jit_solution(17675708196262699032)
XLA Ops:
  0.6 35.6 %shard_map.94 = (bf16[1536,128]{1,0:T(8,128)(2,1)}, bf16[96,128]{1,0:T(8,128)(2,1)}, bf16[96,128]{1,0:T(8,128)(2,1)}) custom-call(s32[16]{0:T(128)} %span_ref.1, bf16[1536,128]{1,0:T(8,128)(2,1)} %bitcast.10, bf16[96,128]{1,0:T(8,128)(2,1)} %bitcast.15, bf16[96,128]{1,0:T(8,128)(2,1)} %bitcast.16, bf16[1536,128]{1,0:T(8,128)(2,1)} %bitcast.11, ...), custom_call_target="tpu_custom_call" | custom-call | tf_op jit(solution)/shard_map/pallas_call | solution.py:247
  36.2 0.0 copy-start.1
  36.3 1.8 %copy.13 = bf16[96,16,128]{2,1,0:T(8,128)(2,1)} copy(bf16[96,16,128]{2,1,0:T(8,128)(2,1)} %bitcast.9) | data formatting | bytes 786432
  38.0 0.0 copy-done.1
  38.0 0.0 copy-start
  38.0 0.6 %copy.14 = bf16[96,1,128]{2,0,1:T(8,128)(2,1)} copy(bf16[96,1,128]{2,0,1:T(8,128)(2,1)S(1)} %bitcast.14) | data formatting | bytes 49152
  38.6 0.1 copy-done
  38.8 0.6 %copy.15 = bf16[96,1,128]{2,0,1:T(8,128)(2,1)} copy(bf16[96,1,128]{2,0,1:T(8,128)(2,1)S(1)} %bitcast.13) | data formatting | bytes 49152
Async XLA Ops:
  36.2 1.8 %copy-start.1 = (bf16[96,128]{1,0:T(8,128)(2,1)S(1)}, bf16[96,128]{1,0:T(8,128)(2,1)}, u32[]{:S(2)}) copy-start(bf16[96,128]{1,0:T(8,128)(2,1)} %get-tuple-element.7) | copy-start | bytes 73732
  38.0 0.7 %copy-start = (bf16[96,128]{1,0:T(8,128)(2,1)S(1)}, bf16[96,128]{1,0:T(8,128)(2,1)}, u32[]{:S(2)}) copy-start(bf16[96,128]{1,0:T(8,128)(2,1)} %get-tuple-element.8) | copy-start | bytes 73732
